TPU v7x, 32 devices: a whole 2x2x4 slice. The times are simulated.
32 devices in a mesh: seq: 16 (over z, x, core), head: 2 (over y).
Axes of the slice: x: 2, y: 2, z: 4, core: 2. Of those that a mesh axis runs over, the one named last changes fastest.
Arguments:
- queries: bfloat16 [8192, 4096], P(('seq', 'head')), may hold values from -8 to 8
- keys: bfloat16 [8192, 2048], P(('seq', 'head')), may hold values from -8 to 8
- values: bfloat16 [8192, 2048], P(('seq', 'head')), may hold values from -6 to 6
- output_cotangent: bfloat16 [8192, 4096], P(('seq', 'head')), may hold values from -6 to 6
Outputs:
- attended: bfloat16 [8192, 4096], P(('seq', 'head'))
- grad_queries: bfloat16 [8192, 4096], P(('seq', 'head'))
- key_gradient: bfloat16 [8192, 2048], P(('seq', 'head'))
- value_gradient: bfloat16 [8192, 2048], P(('seq', 'head'))
All inputs are finite; a program needn't handle non-finite values.
Results may differ from a plain program's by a relative error of at most 0.0095.
Values may be sent and summed in bfloat16 or wider, within the bound.
A program may use at most 128 MiB of HBM per device.

v0:
```python
import jax
import jax.numpy as jnp
from jax import lax
from jax.sharding import PartitionSpec as P

HEAD_SIZE = 128
WINDOW_TOKENS = 1024


query_scale = 168.0 ** (-0.5)


def passed_along(value, axis, steps):
    count = lax.axis_size(axis)
    leading, last = (max(0, -steps), min(count, count - steps))
    return lax.ppermute(value, axis, [(source, source + steps) for source in range(leading, last)])


def mix(form, left, right):
    return jnp.einsum(form, left, right, preferred_element_type=jnp.float32)


def head_pass(query_head, key_extended, value_extended, grad_head, start, block):
    group_factor, total_count, width = query_head.shape
    steps = total_count // block
    rows = jnp.arange(block, dtype=jnp.int32)[:, None]
    cols = jnp.arange(WINDOW_TOKENS + block, dtype=jnp.int32)[None, :]

    def visit(carry, index):
        dk_acc, dv_acc = carry
        anchor = index * block
        key_pos = start + anchor + cols - WINDOW_TOKENS
        allowed = (cols > rows) & (cols <= rows + WINDOW_TOKENS) & (key_pos >= 0)
        scores = query_scale * mix("rqd,kd->rqk", query_head, key_extended)
        scores = jnp.where(allowed[None], scores, -1e30)
        top = jnp.max(scores, axis=-1, keepdims=True)
        lse = top + jnp.log(jnp.sum(jnp.exp(scores - top), axis=-1, keepdims=True))
        probs = jnp.exp(scores - lse)
        probs_b = probs.astype(jnp.bfloat16)
        out_b = mix("rqk,kd->rqd", probs_b, value_extended).astype(jnp.bfloat16)
        delta = jnp.sum(grad_head.astype(jnp.float32) * out_b.astype(jnp.float32), axis=-1)
        dprobs = mix("rqd,kd->rqk", grad_head, value_extended)
        dscores = (probs * (dprobs - delta[..., None])).astype(jnp.bfloat16)
        dq_b = (query_scale * mix("rqk,kd->rqd", dscores, key_extended)).astype(jnp.bfloat16)
        dk_slab = query_scale * mix("rqk,rqd->kd", dscores, query_head)
        dv_slab = mix("rqk,rqd->kd", probs_b, grad_head)
        dk_acc = dk_acc + dk_slab
        dv_acc = dv_acc + dv_slab
        return ((dk_acc, dv_acc), (out_b, dq_b))

    empty = jnp.zeros((WINDOW_TOKENS + total_count, width), jnp.float32)
    (dk_acc, dv_acc), (outs, grads) = lax.scan(
        visit, (empty, empty), jnp.arange(steps, dtype=jnp.int32)
    )
    outs = outs.transpose(1, 0, 2, 3).reshape(group_factor, total_count, width)
    grads = grads.transpose(1, 0, 2, 3).reshape(group_factor, total_count, width)
    return (outs, grads, dk_acc, dv_acc)


def body(queries, keys, values, output_cotangent):
    length = queries.shape[0] * lax.axis_size("head")
    hops = max(1, WINDOW_TOKENS // length)
    span = min(WINDOW_TOKENS, length)
    q_loc, k_loc, v_loc, g_loc = (
        lax.all_to_all(queries, "head", split_axis=1, concat_axis=0, tiled=True),
        lax.all_to_all(keys, "head", split_axis=1, concat_axis=0, tiled=True),
        lax.all_to_all(values, "head", split_axis=1, concat_axis=0, tiled=True),
        lax.all_to_all(output_cotangent, "head", split_axis=1, concat_axis=0, tiled=True),
    )
    key_parts = []
    value_parts = []
    for hop in range(hops, 0, -1):
        key_far, value_far = passed_along((k_loc, v_loc), "seq", hop)
        key_parts.append(key_far)
        value_parts.append(value_far)
    key_halo = jnp.concatenate(key_parts, 0)
    value_halo = jnp.concatenate(value_parts, 0)
    width = HEAD_SIZE
    groups = k_loc.shape[1] // width
    group_factor = q_loc.shape[1] // width // groups
    start = lax.axis_index("seq") * length
    query_head_rows = q_loc.reshape(length, groups, group_factor, width).transpose(1, 2, 0, 3)
    head_gradients = g_loc.reshape(length, groups, group_factor, width).transpose(1, 2, 0, 3)
    key_extended = (
        jnp.concatenate([key_halo, k_loc], 0)
        .reshape(WINDOW_TOKENS + length, groups, width)
        .transpose(1, 0, 2)
    )
    value_extended = (
        jnp.concatenate([value_halo, v_loc], 0)
        .reshape(WINDOW_TOKENS + length, groups, width)
        .transpose(1, 0, 2)
    )
    block = min(512, length)

    def per_head(parts):
        return head_pass(parts[0], parts[1], parts[2], parts[3], start, block)

    outs, grads_q, key_grad_parts, value_grad_parts = lax.map(
        per_head, (query_head_rows, key_extended, value_extended, head_gradients)
    )
    out_loc = outs.transpose(2, 0, 1, 3).reshape(length, groups * group_factor * width)
    dq_loc = grads_q.transpose(2, 0, 1, 3).reshape(length, groups * group_factor * width)
    dk_ext = key_grad_parts.transpose(1, 0, 2).reshape(WINDOW_TOKENS + length, groups * width)
    dv_ext = value_grad_parts.transpose(1, 0, 2).reshape(WINDOW_TOKENS + length, groups * width)
    tail_k = dk_ext[WINDOW_TOKENS + length - span :]
    tail_v = dv_ext[WINDOW_TOKENS + length - span :]
    for hop in range(1, hops + 1):
        offset = (hops - hop) * span
        back_k, back_v = passed_along(
            (dk_ext[offset : offset + span], dv_ext[offset : offset + span]), "seq", -hop
        )
        tail_k = tail_k + back_k
        tail_v = tail_v + back_v
    dk_loc = jnp.concatenate(
        [dk_ext[WINDOW_TOKENS : WINDOW_TOKENS + length - span], tail_k], 0
    ).astype(jnp.bfloat16)
    dv_loc = jnp.concatenate(
        [dv_ext[WINDOW_TOKENS : WINDOW_TOKENS + length - span], tail_v], 0
    ).astype(jnp.bfloat16)
    attended, grad_queries, key_gradient, value_gradient = (
        lax.all_to_all(out_loc, "head", split_axis=0, concat_axis=1, tiled=True),
        lax.all_to_all(dq_loc, "head", split_axis=0, concat_axis=1, tiled=True),
        lax.all_to_all(dk_loc, "head", split_axis=0, concat_axis=1, tiled=True),
        lax.all_to_all(dv_loc, "head", split_axis=0, concat_axis=1, tiled=True),
    )
    return (attended, grad_queries, key_gradient, value_gradient)


def solution(mesh):
    return jax.shard_map(
        body,
        mesh=mesh,
        in_specs=(
            P(("seq", "head"), None),
            P(("seq", "head"), None),
            P(("seq", "head"), None),
            P(("seq", "head"), None),
        ),
        out_specs=(
            P(("seq", "head"), None),
            P(("seq", "head"), None),
            P(("seq", "head"), None),
            P(("seq", "head"), None),
        ),
        check_vma=False,
    )
```

profile of v0, /device:TPU:15, one launch (start us, length us, event | category | flops | bytes accessed | tf_op | source)
XLA Modules:
  0.0 461.4 jit_solution(2532012808601558124)
XLA Ops:
  3.0 3.8 all-to-all-start.1
  8.1 10.6 %all-to-all-done.1 = bf16[256,2,1024]{0,2,1:T(8,128)(2,1)S(1)} async-done(((bf16[256,2,1024]{0,2,1:T(8,128)(2,1)}), bf16[256,2,1024]{0,2,1:T(8,128)(2,1)S(1)}, u32[]{:S(2)}, u32[]{:S(2)}) %all-to-all-start.1) | async-done | bytes 1048608 | tf_op jit(solution)/shard_map/all_to_all | solution.py:66
  18.7 4.7 %all-to-all-start.2 = ((bf16[256,2,1024]{0,2,1:T(8,128)(2,1)}), bf16[256,2,1024]{0,2,1:T(8,128)(2,1)S(1)}, u32[]{:S(2)}, u32[]{:S(2)}) async-start(bf16[256,2,1024]{0,2,1:T(8,128)(2,1)} %bitcast.21), calls=%async_computation.2 | async-start | bytes 2097152 | tf_op jit(solution)/shard_map/all_to_all | solution.py:67
  23.4 3.2 copy.156
  26.5 7.7 %all-to-all-done.2 = bf16[256,2,1024]{0,2,1:T(8,128)(2,1)S(1)} async-done(((bf16[256,2,1024]{0,2,1:T(8,128)(2,1)}), bf16[256,2,1024]{0,2,1:T(8,128)(2,1)S(1)}, u32[]{:S(2)}, u32[]{:S(2)}) %all-to-all-start.2) | async-done | bytes 1048608 | tf_op jit(solution)/shard_map/all_to_all | solution.py:67
  35.2 4.9 %all-to-all-start = ((bf16[256,2,2048]{2,0,1:T(8,128)(2,1)}), bf16[256,2,2048]{2,0,1:T(8,128)(2,1)S(1)}, u32[]{:S(2)}, u32[]{:S(2)}) async-start(bf16[256,2,2048]{2,0,1:T(8,128)(2,1)} %bitcast.156), calls=%async_computation | async-start | bytes 4194304 | tf_op jit(solution)/shard_map/all_to_all | solution.py:65
  40.2 4.1 copy.109
  44.3 17.1 %all-to-all-done = bf16[256,2,2048]{2,0,1:T(8,128)(2,1)S(1)} async-done(((bf16[256,2,2048]{2,0,1:T(8,128)(2,1)}), bf16[256,2,2048]{2,0,1:T(8,128)(2,1)S(1)}, u32[]{:S(2)}, u32[]{:S(2)}) %all-to-all-start) | async-done | bytes 2097184 | tf_op jit(solution)/shard_map/all_to_all | solution.py:65
  61.4 6.0 %all-to-all-start.3 = ((bf16[256,2,2048]{0,2,1:T(8,128)(2,1)}), bf16[256,2,2048]{0,2,1:T(8,128)(2,1)}, u32[]{:S(2)}, u32[]{:S(2)}) async-start(bf16[256,2,2048]{0,2,1:T(8,128)(2,1)} %bitcast.155), calls=%async_computation.3 | async-start | bytes 4194304 | tf_op jit(solution)/shard_map/all_to_all | solution.py:68
  69.7 6.7 %collective-permute-start.3 = (bf16[512,1024]{1,0:T(8,128)(2,1)}, bf16[512,1024]{1,0:T(8,128)(2,1)}, u32[]{:S(2)}, u32[]{:S(2)}) collective-permute-start(bf16[512,1024]{1,0:T(8,128)(2,1)} %bitcast.161), channel_id=1, source_target_pairs={{0,2},{2,4},{4,6},{6,8},{8,10},{10,12},{12,14},{14,16},{16,18},{18... | collective-permute-start | bytes 3145736 | tf_op jit(solution)/shard_map/ppermute | solution.py:16
  76.4 3.1 collective-permute-start.2
  83.0 3.2 collective-permute-start
  103.3 17.2 %collective-permute-done.2 = bf16[512,1024]{1,0:T(8,128)(2,1)} collective-permute-done((bf16[512,1024]{1,0:T(8,128)(2,1)}, bf16[512,1024]{1,0:T(8,128)(2,1)}, u32[]{:S(2)}, u32[]{:S(2)}) %collective-permute-start.2) | collective-permute-done | bytes 1048608 | tf_op jit(solution)/shard_map/ppermute | solution.py:16
  122.0 15.6 %maximum_bitcast_fusion.1 = bf16[8,1536,128]{2,0,1:T(8,128)(2,1)S(1)} fusion(bf16[512,8,128]{2,1,0:T(8,128)(2,1)S(1)} %bitcast.169, bf16[512,8,128]{2,1,0:T(8,128)(2,1)S(1)} %bitcast.170, bf16[512,8,128]{2,1,0:T(8,128)(2,1)S(1)} %bitcast.172), kind=kLoop, calls=%fused_computation.43 | loop fusion | flops 3145728 | bytes 6291456 | tf_op jit(solution)/shard_map/transpose | solution.py:92
  137.6 3.3 copy.114
  148.6 149.9 %while.19 = (s32[]{:T(128)}, bf16[8,2,512,128]{2,3,1,0:T(8,128)(2,1)}, bf16[8,2,512,128]{3,2,1,0:T(8,128)(2,1)}, f32[8,1536,128]{1,2,0:T(8,128)}, f32[8,1536,128...) while((s32[]{:T(128)}, ...), condition=%wide.region_4.5_spmd, body=%wide.region_0.4_spmd.sunk | while | flops 2440629248 | bytes 52745356 | solution.py:99
  298.4 5.7 %fusion.30 = (f32[512,8,128]{0,2,1:T(8,128)}, f32[512,8,128]{0,2,1:T(8,128)}, f32[512,8,128]{0,2,1:T(8,128)}) fusion(f32[1536,8,128]{0,2,1:T(8,128)} %bitcast.159), kind=kLoop, calls=%fused_computation.52 | loop fusion | bytes 12582912 | tf_op jit(solution)/shard_map/slice | solution.py:107
  311.7 4.6 copy.137
  316.3 3.8 all-to-all-start.4
  320.1 5.7 %fusion.31 = (f32[512,8,128]{0,2,1:T(8,128)}, f32[512,8,128]{0,2,1:T(8,128)}, f32[512,8,128]{0,2,1:T(8,128)}) fusion(f32[1536,8,128]{0,2,1:T(8,128)} %bitcast.160), kind=kLoop, calls=%fused_computation.53 | loop fusion | bytes 12582912 | tf_op jit(solution)/shard_map/slice | solution.py:106
  330.7 5.1 %copy.118 = bf16[512,8,2,128]{3,2,1,0:T(2,128)(2,1)} copy(bf16[512,8,2,128]{3,0,2,1:T(8,128)(2,1)} %bitcast.32) | data formatting | bytes 4194304 | tf_op jit(solution)/shard_map/transpose | solution.py:103
  335.8 4.5 all_to_all.126
  343.0 6.5 %all-to-all-start.5 = ((bf16[2,256,2048]{2,1,0:T(8,128)(2,1)}), bf16[2,256,2048]{2,1,0:T(8,128)(2,1)}, u32[]{:S(2)}, u32[]{:S(2)}) async-start(bf16[2,256,2048]{2,1,0:T(8,128)(2,1)} %all_to_all.126), calls=%async_computation.5 | async-start | bytes 4194304 | tf_op jit(solution)/shard_map/all_to_all | solution.py:123
  349.5 5.2 %collective-permute-done.7 = f32[512,1024]{0,1:T(8,128)} collective-permute-done((f32[512,1024]{0,1:T(8,128)}, f32[512,1024]{0,1:T(8,128)}, u32[]{:S(2)}, u32[]{:S(2)}) %collective-permute-start.7) | collective-permute-done | bytes 2097184 | tf_op jit(solution)/shard_map/ppermute | solution.py:16
  354.7 27.7 %collective-permute-done.6 = f32[512,1024]{0,1:T(8,128)} collective-permute-done((f32[512,1024]{0,1:T(8,128)}, f32[512,1024]{0,1:T(8,128)}, u32[]{:S(2)}, u32[]{:S(2)}) %collective-permute-start.6) | collective-permute-done | bytes 2097184 | tf_op jit(solution)/shard_map/ppermute | solution.py:16
  382.4 3.5 fusion.26
  387.1 4.4 all-to-all-start.7
  391.6 8.4 %collective-permute-done.5 = f32[512,1024]{0,1:T(8,128)} collective-permute-done((f32[512,1024]{0,1:T(8,128)}, f32[512,1024]{0,1:T(8,128)}, u32[]{:S(2)}, u32[]{:S(2)}) %collective-permute-start.5) | collective-permute-done | bytes 2097184 | tf_op jit(solution)/shard_map/ppermute | solution.py:16
  399.9 36.0 %collective-permute-done.4 = f32[512,1024]{0,1:T(8,128)} collective-permute-done((f32[512,1024]{0,1:T(8,128)}, f32[512,1024]{0,1:T(8,128)}, u32[]{:S(2)}, u32[]{:S(2)}) %collective-permute-start.4) | collective-permute-done | bytes 2097184 | tf_op jit(solution)/shard_map/ppermute | solution.py:16
  435.9 3.5 fusion.28
  440.7 3.6 all-to-all-start.6
  446.8 4.1 copy.126
  (178 shorter events, 216.9 us)
Async XLA Ops:
  0.6 6.2 %copy-start.3 = (bf16[256,2048]{1,0:T(8,128)(2,1)S(1)}, bf16[256,2048]{1,0:T(8,128)(2,1)}, u32[]{:S(2)}) copy-start(bf16[256,2048]{1,0:T(8,128)(2,1)} %param.8) | copy-start | bytes 3145732
  3.0 15.7 %all-to-all-start.1 = ((bf16[256,2,1024]{0,2,1:T(8,128)(2,1)}), bf16[256,2,1024]{0,2,1:T(8,128)(2,1)S(1)}, u32[]{:S(2)}, u32[]{:S(2)}) async-start(bf16[256,2,1024]{0,2,1:T(8,128)(2,1)} %bitcast.15), calls=%async_computation.1 | async-start | bytes 2097152 | tf_op jit(solution)/shard_map/all_to_all | solution.py:66
  18.7 15.6 %all-to-all-start.2 = ((bf16[256,2,1024]{0,2,1:T(8,128)(2,1)}), bf16[256,2,1024]{0,2,1:T(8,128)(2,1)S(1)}, u32[]{:S(2)}, u32[]{:S(2)}) async-start(bf16[256,2,1024]{0,2,1:T(8,128)(2,1)} %bitcast.21), calls=%async_computation.2 | async-start | bytes 2097152 | tf_op jit(solution)/shard_map/all_to_all | solution.py:67
  34.3 1.0 copy-start
  35.2 26.1 %all-to-all-start = ((bf16[256,2,2048]{2,0,1:T(8,128)(2,1)}), bf16[256,2,2048]{2,0,1:T(8,128)(2,1)S(1)}, u32[]{:S(2)}, u32[]{:S(2)}) async-start(bf16[256,2,2048]{2,0,1:T(8,128)(2,1)} %bitcast.156), calls=%async_computation | async-start | bytes 4194304 | tf_op jit(solution)/shard_map/all_to_all | solution.py:65
  61.4 34.7 %all-to-all-start.3 = ((bf16[256,2,2048]{0,2,1:T(8,128)(2,1)}), bf16[256,2,2048]{0,2,1:T(8,128)(2,1)}, u32[]{:S(2)}, u32[]{:S(2)}) async-start(bf16[256,2,2048]{0,2,1:T(8,128)(2,1)} %bitcast.155), calls=%async_computation.3 | async-start | bytes 4194304 | tf_op jit(solution)/shard_map/all_to_all | solution.py:68
  69.7 32.0 %collective-permute-start.3 = (bf16[512,1024]{1,0:T(8,128)(2,1)}, bf16[512,1024]{1,0:T(8,128)(2,1)}, u32[]{:S(2)}, u32[]{:S(2)}) collective-permute-start(bf16[512,1024]{1,0:T(8,128)(2,1)} %bitcast.161), channel_id=1, source_target_pairs={{0,2},{2,4},{4,6},{6,8},{8,10},{10,12},{12,14},{14,16},{16,18},{18... | collective-permute-start | bytes 3145736 | tf_op jit(solution)/shard_map/ppermute | solution.py:16
  76.4 44.1 %collective-permute-start.2 = (bf16[512,1024]{1,0:T(8,128)(2,1)}, bf16[512,1024]{1,0:T(8,128)(2,1)}, u32[]{:S(2)}, u32[]{:S(2)}) collective-permute-start(bf16[512,1024]{1,0:T(8,128)(2,1)} %bitcast.162), channel_id=1, source_target_pairs={{0,4},{2,6},{4,8},{6,10},{8,12},{10,14},{12,16},{14,18},{16,20},{1... | collective-permute-start | bytes 3145736 | tf_op jit(solution)/shard_map/ppermute | solution.py:16
  80.8 60.1 %collective-permute-start.1 = (bf16[512,1024]{1,0:T(8,128)(2,1)}, bf16[512,1024]{1,0:T(8,128)(2,1)}, u32[]{:S(2)}, u32[]{:S(2)}) collective-permute-start(bf16[512,1024]{1,0:T(8,128)(2,1)} %bitcast.176), channel_id=1, source_target_pairs={{0,2},{2,4},{4,6},{6,8},{8,10},{10,12},{12,14},{14,16},{16,18},{18... | collective-permute-start | bytes 3145736 | tf_op jit(solution)/shard_map/ppermute | solution.py:16
  83.0 62.2 %collective-permute-start = (bf16[512,1024]{1,0:T(8,128)(2,1)}, bf16[512,1024]{1,0:T(8,128)(2,1)}, u32[]{:S(2)}, u32[]{:S(2)}) collective-permute-start(bf16[512,1024]{1,0:T(8,128)(2,1)} %bitcast.177), channel_id=1, source_target_pairs={{0,4},{2,6},{4,8},{6,10},{8,12},{10,14},{12,16},{14,18},{16,20},{1... | collective-permute-start | bytes 3145736 | tf_op jit(solution)/shard_map/ppermute | solution.py:16
  101.7 20.3 %copy-start.2 = (bf16[64,8,8,128]{3,2,1,0:T(8,128)(2,1)S(1)}, bf16[64,8,8,128]{3,2,1,0:T(8,128)(2,1)}, u32[]{:S(2)}) copy-start(bf16[64,8,8,128]{3,2,1,0:T(8,128)(2,1)} %copy.149) | copy-start | bytes 3145732
  140.9 5.8 %copy-start.1 = (bf16[512,8,128]{0,2,1:T(8,128)(2,1)S(1)}, bf16[512,8,128]{0,2,1:T(8,128)(2,1)}, u32[]{:S(2)}) copy-start(bf16[512,8,128]{0,2,1:T(8,128)(2,1)} %reshape.144) | copy-start | bytes 3145732
  304.2 50.5 %collective-permute-start.7 = (f32[512,1024]{0,1:T(8,128)}, f32[512,1024]{0,1:T(8,128)}, u32[]{:S(2)}, u32[]{:S(2)}) collective-permute-start(f32[512,1024]{0,1:T(8,128)} %bitcast.45), channel_id=1, source_target_pairs={{4,0},{6,2},{8,4},{10,6},{12,8},{14,10},{16,12},{18,14},{20,16},{2... | collective-permute-start | bytes 6291464 | tf_op jit(solution)/shard_map/ppermute | solution.py:16
  307.2 75.1 %collective-permute-start.6 = (f32[512,1024]{0,1:T(8,128)}, f32[512,1024]{0,1:T(8,128)}, u32[]{:S(2)}, u32[]{:S(2)}) collective-permute-start(f32[512,1024]{0,1:T(8,128)} %bitcast.44), channel_id=1, source_target_pairs={{2,0},{4,2},{6,4},{8,6},{10,8},{12,10},{14,12},{16,14},{18,16},{20... | collective-permute-start | bytes 6291464 | tf_op jit(solution)/shard_map/ppermute | solution.py:16
  316.3 26.7 %all-to-all-start.4 = ((bf16[2,256,2048]{2,1,0:T(8,128)(2,1)}), bf16[2,256,2048]{2,1,0:T(8,128)(2,1)S(1)}, u32[]{:S(2)}, u32[]{:S(2)}) async-start(bf16[2,256,2048]{2,1,0:T(8,128)(2,1)} %copy.137), calls=%async_computation.4 | async-start | bytes 4194304 | tf_op jit(solution)/shard_map/all_to_all | solution.py:122
  325.8 74.2 %collective-permute-start.5 = (f32[512,1024]{0,1:T(8,128)}, f32[512,1024]{0,1:T(8,128)}, u32[]{:S(2)}, u32[]{:S(2)}) collective-permute-start(f32[512,1024]{0,1:T(8,128)} %bitcast.38), channel_id=1, source_target_pairs={{4,0},{6,2},{8,4},{10,6},{12,8},{14,10},{16,12},{18,14},{20,16},{2... | collective-permute-start | bytes 6291464 | tf_op jit(solution)/shard_map/ppermute | solution.py:16
  327.9 108.1 %collective-permute-start.4 = (f32[512,1024]{0,1:T(8,128)}, f32[512,1024]{0,1:T(8,128)}, u32[]{:S(2)}, u32[]{:S(2)}) collective-permute-start(f32[512,1024]{0,1:T(8,128)} %bitcast.37), channel_id=1, source_target_pairs={{2,0},{4,2},{6,4},{8,6},{10,8},{12,10},{14,12},{16,14},{18,16},{20... | collective-permute-start | bytes 6291464 | tf_op jit(solution)/shard_map/ppermute | solution.py:16
  343.0 44.2 %all-to-all-start.5 = ((bf16[2,256,2048]{2,1,0:T(8,128)(2,1)}), bf16[2,256,2048]{2,1,0:T(8,128)(2,1)}, u32[]{:S(2)}, u32[]{:S(2)}) async-start(bf16[2,256,2048]{2,1,0:T(8,128)(2,1)} %all_to_all.126), calls=%async_computation.5 | async-start | bytes 4194304 | tf_op jit(solution)/shard_map/all_to_all | solution.py:123
  387.1 53.6 %all-to-all-start.7 = ((bf16[2,256,1024]{2,1,0:T(8,128)(2,1)}), bf16[2,256,1024]{2,1,0:T(8,128)(2,1)}, u32[]{:S(2)}, u32[]{:S(2)}) async-start(bf16[2,256,1024]{2,1,0:T(8,128)(2,1)} %bitcast.164), calls=%async_computation.7 | async-start | bytes 2097152 | tf_op jit(solution)/shard_map/all_to_all | solution.py:125
  440.7 18.8 %all-to-all-start.6 = ((bf16[2,256,1024]{2,1,0:T(8,128)(2,1)}), bf16[2,256,1024]{2,1,0:T(8,128)(2,1)S(1)}, u32[]{:S(2)}, u32[]{:S(2)}) async-start(bf16[2,256,1024]{2,1,0:T(8,128)(2,1)} %bitcast.165), calls=%async_computation.6 | async-start | bytes 2097152 | tf_op jit(solution)/shard_map/all_to_all | solution.py:124
where the time goes:
time: 465 us; the launch traced here: 461 us
  waiting for transfers between devices  135 us (29%)
  matrix products  113 us (24%)
  local copies, waits for them, and re-layouts  110 us (24%)
  starting transfers between devices  62.8 us (14%)
  other arithmetic  38.5 us (8%)
    dot_general x48, matrix products, mix(): return jnp.einsum(form, left, right, preferred_element_type=jnp.float32)  113 us
    ppermute x8, waiting for transfers between devices, passed_along(): lax.ppermute(value, axis, [(source, source + steps) for source in range(l...  97.2 us
    ppermute x8, starting transfers between devices, passed_along(): lax.ppermute(value, axis, [(source, source + steps) for source in range(l...  25.1 us
    unnamed x18, local copies, waits for them, and re-layouts  24.1 us
    all_to_all x1, waiting for transfers between devices, body(): lax.all_to_all(queries, 'head', split_axis=1, concat_axis=0, tiled=True)  17.1 us
    transpose x1, other arithmetic, body(): value_extended = jnp.concatenate([value_halo, v_loc], 0).reshape(WINDOW_T...  15.6 us
    dynamic_slice x16, local copies, waits for them, and re-layouts, body(): lax.map(per_head, (query_head_rows, key_extended, value_extended, head_gr...  12.5 us
    all_to_all x1, waiting for transfers between devices, body(): lax.all_to_all(keys, 'head', split_axis=1, concat_axis=0, tiled=True)  10.6 us
  transfers between devices with their start and end apart: 16, of which 10 were waited for; matrix products, arithmetic and copies ran while one was open for 20% of the time, Pallas kernels for 0%

commit v1 on v0

v1 whole, which is shorter than its diff:
```python
import functools

import jax
import jax.numpy as jnp
from jax import lax
from jax.experimental import pallas as pl
from jax.experimental.pallas import tpu as pltpu
from jax.sharding import PartitionSpec as P

HEAD_SIZE = 128
WINDOW_TOKENS = 1024
TILE = 256
MESH = pl.DeviceIdType.MESH

query_scale = 168.0 ** (-0.5)
exponent_scale = query_scale * 1.4426950408889634
HIDDEN = -1e30


def matmul(left, right):
    return jnp.dot(left, right, preferred_element_type=jnp.float32)


def matmul_nt(left, right):
    return lax.dot_general(left, right, (((1,), (1,)), ((), ())), preferred_element_type=jnp.float32)


def turned(value):
    return value.astype(jnp.float32).T


def attend(n, factor, first, qb, gb, kb, vb, kt, vt, ob, dqb, dk, dv):
    width = HEAD_SIZE
    chunks = WINDOW_TOKENS // TILE
    dk[n] = jnp.zeros(dk.shape[1:], jnp.float32)
    dv[n] = jnp.zeros(dv.shape[1:], jnp.float32)

    def turn(at, _):
        row = pl.multiple_of(at * TILE, TILE)
        kt[:, pl.ds(row, TILE)] = turned(kb[n, pl.ds(row, TILE), :]).astype(jnp.bfloat16)
        vt[:, pl.ds(row, TILE)] = turned(vb[n, pl.ds(row, TILE), :]).astype(jnp.bfloat16)
        return 0

    lax.fori_loop(0, kb.shape[1] // TILE, turn, 0)
    key_at = lax.broadcasted_iota(jnp.int32, (TILE, TILE), 0)
    query_at = lax.broadcasted_iota(jnp.int32, (TILE, TILE), 1)

    def block(at, _):
        row = pl.multiple_of(at * TILE, TILE)
        rows = [pl.ds(pl.multiple_of(row + c * TILE, TILE), TILE) for c in range(chunks + 1)]
        shift = [
            jnp.where(jnp.logical_and(first, at + c < chunks), -HIDDEN, 0.0) for c in range(chunks)
        ] + [0.0]
        queries, grads, probs, rounded, deltas = [], [], [], [], []
        for r in range(factor):
            q = qb[n, pl.ds(row, TILE), r * width : (r + 1) * width]
            g = gb[n, pl.ds(row, TILE), r * width : (r + 1) * width]
            scores = []
            for c in range(chunks + 1):
                s = matmul_nt(kb[n, rows[c], :], q)
                if c == 0:
                    s = jnp.where(key_at > query_at, s, HIDDEN)
                if c == chunks:
                    s = jnp.where(key_at <= query_at, s, HIDDEN)
                scores.append(s)
            top = None
            for c in range(chunks + 1):
                most = jnp.max(scores[c], axis=0, keepdims=True) - shift[c]
                top = most if top is None else jnp.maximum(top, most)
            total = None
            powers = []
            for c in range(chunks + 1):
                e = jnp.exp2(scores[c] * exponent_scale - (top + shift[c]) * exponent_scale)
                part = jnp.sum(e, axis=0, keepdims=True)
                total = part if total is None else total + part
                powers.append(e)
            inverse = 1.0 / total
            prob = [e * inverse for e in powers]
            prob_b = [p.astype(jnp.bfloat16) for p in prob]
            out = None
            for c in range(chunks + 1):
                part = matmul(vt[:, rows[c]], prob_b[c])
                out = part if out is None else out + part
            out_b = out.astype(jnp.bfloat16)
            deltas.append(jnp.sum(turned(g) * out_b.astype(jnp.float32), axis=0, keepdims=True))
            ob[n, pl.ds(row, TILE), r * width : (r + 1) * width] = out.T.astype(jnp.bfloat16)
            queries.append(q)
            grads.append(g)
            probs.append(prob)
            rounded.append(prob_b)
        dq = [None] * factor
        for c in range(chunks + 1):
            dk_part, dv_part = None, None
            for r in range(factor):
                dprob = matmul_nt(vb[n, rows[c], :], grads[r])
                ds = (probs[r][c] * (dprob - deltas[r])).astype(jnp.bfloat16)
                part = matmul(kt[:, rows[c]], ds)
                dq[r] = part if dq[r] is None else dq[r] + part
                part = matmul(ds, queries[r])
                dk_part = part if dk_part is None else dk_part + part
                part = matmul(rounded[r][c], grads[r])
                dv_part = part if dv_part is None else dv_part + part
            dk[n, rows[c], :] += dk_part
            dv[n, rows[c], :] += dv_part
        for r in range(factor):
            dqb[n, pl.ds(row, TILE), r * width : (r + 1) * width] = (dq[r] * query_scale).T.astype(jnp.bfloat16)
        return 0

    lax.fori_loop(0, (kb.shape[1] - WINDOW_TOKENS) // TILE, block, 0)


def kernel(
    near, heads, factor, queries, keys, values, cotangent, attended, grad_queries, key_gradient, value_gradient,
    qb, gb, kb, vb, kt, vt, ob, dqb, dk, dv, dk_far, dv_far, dk_back, dv_back, dk_own, dv_own,
    in_send, in_recv, halo_send, halo_recv, back_send, back_recv, out_send, out_recv,
):
    length = queries.shape[0]
    width = HEAD_SIZE
    side = lax.axis_size("head")
    members = near * side
    teams = lax.axis_size("seq") // near
    seq, head = lax.axis_index("seq"), lax.axis_index("head")
    team = seq // near
    me = lax.rem(seq, near) * side + head
    has_before, has_after = team > 0, team < teams - 1

    def device(team_at, member):
        return (team_at * near + member // side, lax.rem(member, side))

    ahead, behind = device(team + 1, me), device(team - 1, me)
    barrier = pltpu.get_barrier_semaphore()
    for d in range(1, members):
        pl.semaphore_signal(barrier, inc=1, device_id=device(team, lax.rem(me + d, members)), device_id_type=MESH)

    @pl.when(has_after)
    def _():
        pl.semaphore_signal(barrier, inc=1, device_id=ahead, device_id_type=MESH)

    @pl.when(has_before)
    def _():
        pl.semaphore_signal(barrier, inc=1, device_id=behind, device_id_type=MESH)

    pl.semaphore_wait(barrier, members - 1 + has_after.astype(jnp.int32) + has_before.astype(jnp.int32))

    def columns(member, n, size):
        return pl.ds(pl.multiple_of((member * heads + n) * size, size), size)

    def token_rows(member, start=0):
        return pl.ds(pl.multiple_of(start + member * length, length), length)

    wide = factor * width
    entering = ((keys, width, kb, WINDOW_TOKENS), (values, width, vb, WINDOW_TOKENS), (queries, wide, qb, 0), (cotangent, wide, gb, 0))
    leaving = ((ob, wide, attended), (dqb, wide, grad_queries), (dk_own, width, key_gradient), (dv_own, width, value_gradient))

    def entry(n, d, a):
        source, size, buffer, start = entering[a]
        other = lax.rem(me + d, members)
        src = source.at[:, columns(other, n, size)]
        dst = buffer.at[n, token_rows(me, start), :]
        if d == 0:
            return pltpu.make_async_copy(src, dst, in_recv.at[n, 0, a])
        return pltpu.make_async_remote_copy(
            src, dst, in_send.at[n, d, a], in_recv.at[n, d, a], device_id=device(team, other), device_id_type=MESH
        )

    def enter(n, which):
        for a in which:
            for d in (*range(1, members), 0):
                entry(n, d, a).start()

    def entered(n, which):
        for a in which:
            entry(n, 0, a).wait()
            for d in range(1, members):
                entry(n, d, a).wait_recv()

    def halo(n, a):
        buffer = entering[a][2]
        return pltpu.make_async_remote_copy(
            buffer.at[n, pl.ds(WINDOW_TOKENS, WINDOW_TOKENS), :], buffer.at[n, pl.ds(0, WINDOW_TOKENS), :],
            halo_send.at[n, a], halo_recv.at[n, a], device_id=ahead, device_id_type=MESH,
        )

    def back(n, a):
        source, target = ((dk_far, dk_back), (dv_far, dv_back))[a]
        return pltpu.make_async_remote_copy(
            source.at[n], target.at[n], back_send.at[n, a], back_recv.at[n, a], device_id=behind, device_id_type=MESH
        )

    def exit_copy(n, d, a):
        buffer, size, target = leaving[a]
        other = lax.rem(me + d, members)
        src = buffer.at[n, token_rows(other), :]
        dst = target.at[:, columns(me, n, size)]
        if d == 0:
            return pltpu.make_async_copy(src, dst, out_recv.at[n, 0, a])
        return pltpu.make_async_remote_copy(
            src, dst, out_send.at[n, d, a], out_recv.at[n, d, a], device_id=device(team, other), device_id_type=MESH
        )

    def leave(n, which):
        for a in which:
            for d in (*range(1, members), 0):
                exit_copy(n, d, a).start()

    def send_halo(n):
        entered(n, (0, 1))

        @pl.when(has_after)
        def _():
            halo(n, 0).start()
            halo(n, 1).start()

    def finish(n):
        for a, (total, received, result, factor_of) in enumerate(
            ((dk, dk_back, dk_own, query_scale), (dv, dv_back, dv_own, 1.0))
        ):
            own = total[n, pl.ds(WINDOW_TOKENS, WINDOW_TOKENS), :] * factor_of

            @pl.when(has_after)
            def _():
                back(n, a).wait_recv()
                result[n] = (own + received[n].astype(jnp.float32)).astype(jnp.bfloat16)

            @pl.when(jnp.logical_not(has_after))
            def _():
                result[n] = own.astype(jnp.bfloat16)

        leave(n, (2, 3))

    @pl.when(jnp.logical_not(has_before))
    def _():
        for n in range(heads):
            kb[n, pl.ds(0, WINDOW_TOKENS), :] = jnp.zeros((WINDOW_TOKENS, width), kb.dtype)
            vb[n, pl.ds(0, WINDOW_TOKENS), :] = jnp.zeros((WINDOW_TOKENS, width), vb.dtype)

    enter(0, (0, 1))
    if heads > 1:
        enter(1, (0, 1))
    enter(0, (2, 3))
    if heads > 2:
        enter(2, (0, 1))
    if heads > 1:
        enter(1, (2, 3))
    send_halo(0)

    def step(n, _):
        @pl.when(n + 1 < heads)
        def _():
            send_halo(n + 1)

        entered(n, (2, 3))

        @pl.when(n + 3 < heads)
        def _():
            enter(n + 3, (0, 1))

        @pl.when(n + 2 < heads)
        def _():
            enter(n + 2, (2, 3))

        @pl.when(has_before)
        def _():
            halo(n, 0).wait_recv()
            halo(n, 1).wait_recv()

        attend(n, factor, jnp.logical_not(has_before), qb, gb, kb, vb, kt, vt, ob, dqb, dk, dv)

        @pl.when(has_before)
        def _():
            dk_far[n] = (dk[n, pl.ds(0, WINDOW_TOKENS), :] * query_scale).astype(jnp.bfloat16)
            dv_far[n] = dv[n, pl.ds(0, WINDOW_TOKENS), :].astype(jnp.bfloat16)
            back(n, 0).start()
            back(n, 1).start()

        leave(n, (0, 1))

        @pl.when(n > 0)
        def _():
            finish(n - 1)

        return 0

    lax.fori_loop(0, heads, step, 0)
    finish(heads - 1)

    def drain(n, _):
        for a in range(4):
            exit_copy(n, 0, a).wait()
            for d in range(1, members):
                entry(n, d, a).wait_send()
                exit_copy(n, d, a).wait()

        @pl.when(has_after)
        def _():
            halo(n, 0).wait_send()
            halo(n, 1).wait_send()

        @pl.when(has_before)
        def _():
            back(n, 0).wait_send()
            back(n, 1).wait_send()

        return 0

    lax.fori_loop(0, heads, drain, 0)


def body(queries, keys, values, output_cotangent):
    length = queries.shape[0]
    side = lax.axis_size("head")
    near = WINDOW_TOKENS // (length * side)
    members = near * side
    width = HEAD_SIZE
    heads = keys.shape[1] // width // members
    factor = queries.shape[1] // keys.shape[1]
    wide = factor * width
    low, high = jnp.bfloat16, jnp.float32
    window = WINDOW_TOKENS
    pairs = heads * 2 * window * TILE * 6 * factor * width
    return tuple(
        pl.pallas_call(
            functools.partial(kernel, near, heads, factor),
            out_shape=[jax.ShapeDtypeStruct(x.shape, x.dtype) for x in (queries, queries, keys, values)],
            in_specs=[pl.BlockSpec(memory_space=pl.ANY)] * 4,
            out_specs=[pl.BlockSpec(memory_space=pl.ANY)] * 4,
            scratch_shapes=[
                pltpu.VMEM((heads, window, wide), low),
                pltpu.VMEM((heads, window, wide), low),
                pltpu.VMEM((heads, 2 * window, width), low),
                pltpu.VMEM((heads, 2 * window, width), low),
                pltpu.VMEM((width, 2 * window), low),
                pltpu.VMEM((width, 2 * window), low),
                pltpu.VMEM((heads, window, wide), low),
                pltpu.VMEM((heads, window, wide), low),
                pltpu.VMEM((heads, 2 * window, width), high),
                pltpu.VMEM((heads, 2 * window, width), high),
                *[pltpu.VMEM((heads, window, width), low)] * 6,
                pltpu.SemaphoreType.DMA((heads, members, 4)),
                pltpu.SemaphoreType.DMA((heads, members, 4)),
                *[pltpu.SemaphoreType.DMA((heads, 2))] * 4,
                pltpu.SemaphoreType.DMA((heads, members, 4)),
                pltpu.SemaphoreType.DMA((heads, members, 4)),
            ],
            compiler_params=pltpu.CompilerParams(
                collective_id=0, has_side_effects=True, vmem_limit_bytes=60 * 1024 * 1024
            ),
            cost_estimate=pl.CostEstimate(flops=pairs * 2, bytes_accessed=24 * queries.size, transcendentals=0),
        )(queries, keys, values, output_cotangent)
    )


def solution(mesh):
    spec = P(("seq", "head"), None)
    return jax.shard_map(
        body,
        mesh=mesh,
        in_specs=(spec,) * 4,
        out_specs=(spec,) * 4,
        check_vma=False,
    )
```

time: 465 us -> 152 us (0.33)
  Pallas kernels: 0 us -> 141 us
  waiting for transfers between devices: 135 us -> 0 us
  matrix products: 113 us -> 0 us
  local copies, waits for them, and re-layouts: 110 us -> 7.81 us
  starting transfers between devices: 62.8 us -> 0 us
  other arithmetic: 38.5 us -> 0 us
    pallas_call x0 -> x1, Pallas kernels: none -> 141 us  [body(): pl.pallas_call(functools.partial(kernel, near, heads, factor), out_shape=...]
    dot_general x48 -> x0, matrix products: 113 us -> none  [mix(): return jnp.einsum(form, left, right, preferred_element_type=jnp.float32)]
    ppermute x8 -> x0, waiting for transfers between devices: 97.2 us -> none  [passed_along(): lax.ppermute(value, axis, [(source, source + steps) for source in range(l...]
    all_to_all x8 -> x0, waiting for transfers between devices: 38.1 us -> none  [the longest x1 17.1 us: body(): lax.all_to_all(queries, 'head', split_axis=1, concat_axis=0, tiled=True)]
    all_to_all x8 -> x0, starting transfers between devices: 37.7 us -> none  [the longest x1 6.54 us: body(): lax.all_to_all(dq_loc, 'head', split_axis=0, concat_axis=1, tiled=True)]
    all_to_all x11 -> x0, local copies, waits for them, and re-layouts: 28.6 us -> none  [the longest x3 9.62 us: body(): lax.all_to_all(out_loc, 'head', split_axis=0, concat_axis=1, tiled=True)]
    ppermute x8 -> x0, starting transfers between devices: 25.1 us -> none  [passed_along(): lax.ppermute(value, axis, [(source, source + steps) for source in range(l...]
    transpose x2 -> x0, other arithmetic: 17.4 us -> none  [the longest x1 15.6 us: body(): value_extended = jnp.concatenate([value_halo, v_loc], 0).reshape(WINDOW_T...]
  transfers between devices with their start and end apart: 16 -> 0, of which waited for: 10 -> 0; matrix products, arithmetic and copies ran while one was open for 20% -> 0% of each run, Pallas kernels for 0% -> 0%
where the time goes in v1:
time: 152 us; the launch traced here: 149 us
  Pallas kernels  141 us (93%)
  local copies, waits for them, and re-layouts  7.81 us (5%)
    pallas_call x1, Pallas kernels, body(): pl.pallas_call(functools.partial(kernel, near, heads, factor), out_shape=...  141 us
    unnamed x10, local copies, waits for them, and re-layouts  7.81 us

profile of v1, /device:TPU:15, one launch (start us, length us, event | category | flops | bytes accessed | tf_op | source)
XLA Modules:
  0.0 149.2 jit_solution(4219346604949345516)
XLA Ops:
  0.6 140.8 %shard_map.75 = (bf16[256,4096]{1,0:T(8,128)(2,1)}, bf16[256,4096]{1,0:T(8,128)(2,1)}, bf16[256,2048]{1,0:T(8,128)(2,1)}, bf16[256,2048]{1,0:T(8,128)(2,1)}) custom-call(bf16[256,4096]{1,0:T(8,128)(2,1)} %queries.1, bf16[256,2048]{1,0:T(8,128)(2,1)} %keys.1, bf16[256,2048]{1,0:T(8,128)(2,1)} %values.1, bf16[256,4096]{1,0:T(8,128)(2,1)} %cotangent.1), custom_call_target="tpu_custom_call" | custom-call | flops 6442450944 | bytes 25165824 | tf_op jit(solution)/shard_map/pallas_call | solution.py:322
  141.4 0.0 copy-start
  141.4 3.3 %copy.12 = bf16[256,4096]{1,0:T(8,128)(2,1)} copy(bf16[256,4096]{1,0:T(8,128)(2,1)} %get-tuple-element.8) | data formatting | bytes 4194304
  144.7 0.0 copy-done
  144.7 0.0 copy-start.2
  144.7 1.3 copy.13
  146.0 0.6 copy-done.2
  146.6 0.0 copy-start.1
  146.6 1.0 copy.14
  147.6 0.6 copy-done.1
  148.2 1.0 copy.15
Async XLA Ops:
  141.4 3.3 %copy-start = (bf16[256,4096]{1,0:T(8,128)(2,1)S(1)}, bf16[256,4096]{1,0:T(8,128)(2,1)}, u32[]{:S(2)}) copy-start(bf16[256,4096]{1,0:T(8,128)(2,1)} %get-tuple-element.9) | copy-start | bytes 6291460
  144.7 2.0 %copy-start.2 = (bf16[256,2048]{1,0:T(8,128)(2,1)S(1)}, bf16[256,2048]{1,0:T(8,128)(2,1)}, u32[]{:S(2)}) copy-start(bf16[256,2048]{1,0:T(8,128)(2,1)} %get-tuple-element.10) | copy-start | bytes 3145732
  146.6 1.6 %copy-start.1 = (bf16[256,2048]{1,0:T(8,128)(2,1)S(1)}, bf16[256,2048]{1,0:T(8,128)(2,1)}, u32[]{:S(2)}) copy-start(bf16[256,2048]{1,0:T(8,128)(2,1)} %get-tuple-element.11) | copy-start | bytes 3145732

commit v2 on v1

v2 whole, which is shorter than its diff:
```python
import functools

import jax
import jax.numpy as jnp
from jax import lax
from jax.experimental import pallas as pl
from jax.experimental.pallas import tpu as pltpu
from jax.sharding import PartitionSpec as P

HEAD_SIZE = 128
WINDOW_TOKENS = 1024
TILE = 256
MESH = pl.DeviceIdType.MESH

query_scale = 168.0 ** (-0.5)
exponent_scale = query_scale * 1.4426950408889634
HIDDEN = -1e30


def matmul(left, right):
    return jnp.dot(left, right, preferred_element_type=jnp.float32)


def matmul_nt(left, right):
    return lax.dot_general(left, right, (((1,), (1,)), ((), ())), preferred_element_type=jnp.float32)


def turned(value):
    return value.astype(jnp.float32).T


def attend(n, factor, first, qb, gb, kb, vb, kt, vt, probs_b, dscores_b, ob, dqb, dk, dv, after_tile):
    width = HEAD_SIZE
    chunks = WINDOW_TOKENS // TILE
    span = WINDOW_TOKENS + TILE
    dk[n] = jnp.zeros(dk.shape[1:], jnp.float32)
    dv[n] = jnp.zeros(dv.shape[1:], jnp.float32)

    def turn(at, _):
        row = pl.multiple_of(at * TILE, TILE)
        kt[:, pl.ds(row, TILE)] = turned(kb[n, pl.ds(row, TILE), :]).astype(jnp.bfloat16)
        vt[:, pl.ds(row, TILE)] = turned(vb[n, pl.ds(row, TILE), :]).astype(jnp.bfloat16)
        return 0

    lax.fori_loop(0, kb.shape[1] // TILE, turn, 0)
    across = factor * TILE
    key_at = lax.broadcasted_iota(jnp.int32, (TILE, across), 0)
    query_at = lax.broadcasted_iota(jnp.int32, (TILE, across), 1) % TILE

    def block(at, _):
        row = pl.multiple_of(at * TILE, TILE)
        slab = pl.ds(row, span)
        rows = [pl.ds(pl.multiple_of(row + c * TILE, TILE), TILE) for c in range(chunks + 1)]
        shift = [
            jnp.where(jnp.logical_and(first, at + c < chunks), -HIDDEN, 0.0) for c in range(chunks)
        ] + [0.0]
        q = jnp.concatenate([qb[n, pl.ds(row, TILE), r * width : (r + 1) * width] for r in range(factor)], 0)
        g = jnp.concatenate([gb[n, pl.ds(row, TILE), r * width : (r + 1) * width] for r in range(factor)], 0)
        scores = []
        for c in range(chunks + 1):
            s = matmul_nt(kb[n, rows[c], :], q)
            if c == 0:
                s = jnp.where(key_at > query_at, s, HIDDEN)
            if c == chunks:
                s = jnp.where(key_at <= query_at, s, HIDDEN)
            scores.append(s)
        top = None
        for c in range(chunks + 1):
            most = jnp.max(scores[c], axis=0, keepdims=True) - shift[c]
            top = most if top is None else jnp.maximum(top, most)
        total = None
        powers = []
        for c in range(chunks + 1):
            e = jnp.exp2(scores[c] * exponent_scale - (top + shift[c]) * exponent_scale)
            part = jnp.sum(e, axis=0, keepdims=True)
            total = part if total is None else total + part
            powers.append(e)
        inverse = 1.0 / total
        probs = [e * inverse for e in powers]
        for c in range(chunks + 1):
            probs_b[c * TILE : (c + 1) * TILE, :] = probs[c].astype(jnp.bfloat16)
        out = matmul(vt[:, slab], probs_b[...])
        out_b = out.astype(jnp.bfloat16).astype(jnp.float32)
        delta = jnp.sum(turned(g) * out_b, axis=0, keepdims=True)
        for r in range(factor):
            ob[n, pl.ds(row, TILE), r * width : (r + 1) * width] = out[:, r * TILE : (r + 1) * TILE].T.astype(jnp.bfloat16)
        for c in range(chunks + 1):
            dprobs = matmul_nt(vb[n, rows[c], :], g)
            dscores_b[c * TILE : (c + 1) * TILE, :] = (probs[c] * (dprobs - delta)).astype(jnp.bfloat16)
        dq = matmul(kt[:, slab], dscores_b[...]) * query_scale
        for c in range(chunks + 1):
            dv[n, rows[c], :] += matmul(probs_b[c * TILE : (c + 1) * TILE, :], g)
            dk[n, rows[c], :] += matmul(dscores_b[c * TILE : (c + 1) * TILE, :], q)
        for r in range(factor):
            dqb[n, pl.ds(row, TILE), r * width : (r + 1) * width] = dq[:, r * TILE : (r + 1) * TILE].T.astype(jnp.bfloat16)
        after_tile(at)
        return 0

    lax.fori_loop(0, (kb.shape[1] - WINDOW_TOKENS) // TILE, block, 0)


def kernel(
    near, heads, factor, queries, keys, values, cotangent, attended, grad_queries, key_gradient, value_gradient,
    qb, gb, kb, vb, kt, vt, probs_b, dscores_b, ob, dqb, dk, dv, dk_far, dv_far, dk_back, dv_back, dk_own, dv_own,
    in_send, in_recv, halo_send, halo_recv, back_send, back_recv, out_send, out_recv,
):
    length = queries.shape[0]
    width = HEAD_SIZE
    side = lax.axis_size("head")
    members = near * side
    teams = lax.axis_size("seq") // near
    seq, head = lax.axis_index("seq"), lax.axis_index("head")
    team = seq // near
    me = lax.rem(seq, near) * side + head
    has_before, has_after = team > 0, team < teams - 1

    def device(team_at, member):
        return (team_at * near + member // side, lax.rem(member, side))

    ahead, behind = device(team + 1, me), device(team - 1, me)
    barrier = pltpu.get_barrier_semaphore()
    for d in range(1, members):
        pl.semaphore_signal(barrier, inc=1, device_id=device(team, lax.rem(me + d, members)), device_id_type=MESH)

    @pl.when(has_after)
    def _():
        pl.semaphore_signal(barrier, inc=1, device_id=ahead, device_id_type=MESH)

    @pl.when(has_before)
    def _():
        pl.semaphore_signal(barrier, inc=1, device_id=behind, device_id_type=MESH)

    pl.semaphore_wait(barrier, members - 1 + has_after.astype(jnp.int32) + has_before.astype(jnp.int32))

    def columns(member, n, size):
        return pl.ds(pl.multiple_of((member * heads + n) * size, size), size)

    def token_rows(member, start=0):
        return pl.ds(pl.multiple_of(start + member * length, length), length)

    wide = factor * width
    entering = ((keys, width, kb, WINDOW_TOKENS), (values, width, vb, WINDOW_TOKENS), (queries, wide, qb, 0), (cotangent, wide, gb, 0))
    leaving = ((ob, wide, attended), (dqb, wide, grad_queries), (dk_own, width, key_gradient), (dv_own, width, value_gradient))

    def entry(n, d, a):
        source, size, buffer, start = entering[a]
        other = lax.rem(me + d, members)
        src = source.at[:, columns(other, n, size)]
        dst = buffer.at[n, token_rows(me, start), :]
        if d == 0:
            return pltpu.make_async_copy(src, dst, in_recv.at[n, 0, a])
        return pltpu.make_async_remote_copy(
            src, dst, in_send.at[n, d, a], in_recv.at[n, d, a], device_id=device(team, other), device_id_type=MESH
        )

    def enter(n, which):
        for a in which:
            for d in (*range(1, members), 0):
                entry(n, d, a).start()

    def entered(n, which):
        for a in which:
            entry(n, 0, a).wait()
            for d in range(1, members):
                entry(n, d, a).wait_recv()

    def halo(n, a):
        buffer = entering[a][2]
        return pltpu.make_async_remote_copy(
            buffer.at[n, pl.ds(WINDOW_TOKENS, WINDOW_TOKENS), :], buffer.at[n, pl.ds(0, WINDOW_TOKENS), :],
            halo_send.at[n, a], halo_recv.at[n, a], device_id=ahead, device_id_type=MESH,
        )

    chunks = WINDOW_TOKENS // TILE

    def back(n, a, c):
        source, target = ((dk_far, dk_back), (dv_far, dv_back))[a]
        rows = pl.ds(pl.multiple_of(c * TILE, TILE), TILE)
        return pltpu.make_async_remote_copy(
            source.at[n, rows, :], target.at[n, rows, :], back_send.at[n, a, c], back_recv.at[n, a, c],
            device_id=behind, device_id_type=MESH,
        )

    def exit_own(n, a):
        buffer, size, target = leaving[a]
        return pltpu.make_async_copy(
            buffer.at[n, token_rows(me), :], target.at[:, columns(me, n, size)], out_recv.at[n, 0, a]
        )

    def exit_copy(n, d, a):
        buffer, size, target = leaving[a]
        other = lax.rem(me + d, members)
        return pltpu.make_async_remote_copy(
            buffer.at[n, token_rows(other), :], target.at[:, columns(me, n, size)],
            out_send.at[n, d, a], out_recv.at[n, d, a], device_id=device(team, other), device_id_type=MESH,
        )

    def leave(n, which):
        for a in which:
            for d in range(1, members):
                exit_copy(n, d, a).start()
            exit_own(n, a).start()

    def send_halo(n):
        entered(n, (0, 1))

        @pl.when(has_after)
        def _():
            halo(n, 0).start()
            halo(n, 1).start()

    def finish(n):
        for a, (total, received, result, factor_of) in enumerate(
            ((dk, dk_back, dk_own, query_scale), (dv, dv_back, dv_own, 1.0))
        ):
            own = total[n, pl.ds(WINDOW_TOKENS, WINDOW_TOKENS), :] * factor_of

            @pl.when(has_after)
            def _():
                for c in range(chunks):
                    back(n, a, c).wait_recv()
                result[n] = (own + received[n].astype(jnp.float32)).astype(jnp.bfloat16)

            @pl.when(jnp.logical_not(has_after))
            def _():
                result[n] = own.astype(jnp.bfloat16)

        leave(n, (2, 3))

    @pl.when(jnp.logical_not(has_before))
    def _():
        for n in range(heads):
            kb[n, pl.ds(0, WINDOW_TOKENS), :] = jnp.zeros((WINDOW_TOKENS, width), kb.dtype)
            vb[n, pl.ds(0, WINDOW_TOKENS), :] = jnp.zeros((WINDOW_TOKENS, width), vb.dtype)

    enter(0, (0, 1))
    if heads > 1:
        enter(1, (0, 1))
    enter(0, (2, 3))
    if heads > 2:
        enter(2, (0, 1))
    if heads > 1:
        enter(1, (2, 3))
    send_halo(0)

    def step(n, _):
        @pl.when(n + 1 < heads)
        def _():
            send_halo(n + 1)

        entered(n, (2, 3))

        @pl.when(n + 3 < heads)
        def _():
            enter(n + 3, (0, 1))

        @pl.when(n + 2 < heads)
        def _():
            enter(n + 2, (2, 3))

        @pl.when(has_before)
        def _():
            halo(n, 0).wait_recv()
            halo(n, 1).wait_recv()

        def after_tile(at):
            @pl.when(has_before)
            def _():
                rows = pl.ds(pl.multiple_of(at * TILE, TILE), TILE)
                dk_far[n, rows, :] = (dk[n, rows, :] * query_scale).astype(jnp.bfloat16)
                dv_far[n, rows, :] = dv[n, rows, :].astype(jnp.bfloat16)
                back(n, 0, at).start()
                back(n, 1, at).start()

            for m in range(TILE // length):
                d = lax.rem(at * (TILE // length) + m - me + members, members)

                @pl.when(d == 0)
                def _():
                    exit_own(n, 0).start()
                    exit_own(n, 1).start()

                @pl.when(d > 0)
                def _():
                    exit_copy(n, d, 0).start()
                    exit_copy(n, d, 1).start()

        attend(
            n, factor, jnp.logical_not(has_before), qb, gb, kb, vb, kt, vt, probs_b, dscores_b, ob, dqb, dk, dv, after_tile
        )

        @pl.when(n > 0)
        def _():
            finish(n - 1)

        return 0

    lax.fori_loop(0, heads, step, 0)
    finish(heads - 1)

    def drain(n, _):
        for a in range(4):
            exit_own(n, a).wait()
            for d in range(1, members):
                entry(n, d, a).wait_send()
                exit_copy(n, d, a).wait()

        @pl.when(has_after)
        def _():
            halo(n, 0).wait_send()
            halo(n, 1).wait_send()

        @pl.when(has_before)
        def _():
            for c in range(chunks):
                back(n, 0, c).wait_send()
                back(n, 1, c).wait_send()

        return 0

    lax.fori_loop(0, heads, drain, 0)


def hand_over(*refs):
    sources, targets, sems = refs[:4], refs[4:8], refs[8]
    parts = sems.shape[1]
    copies = []
    for a in range(4):
        rows = sources[a].shape[0] // parts
        for p in range(parts):
            piece = pl.ds(p * rows, rows)
            copies.append(pltpu.make_async_copy(sources[a].at[piece, :], targets[a].at[piece, :], sems.at[a, p]))
    for copy in copies:
        copy.start()
    for copy in copies:
        copy.wait()


def body(queries, keys, values, output_cotangent):
    length = queries.shape[0]
    side = lax.axis_size("head")
    near = WINDOW_TOKENS // (length * side)
    members = near * side
    width = HEAD_SIZE
    heads = keys.shape[1] // width // members
    factor = queries.shape[1] // keys.shape[1]
    wide = factor * width
    low, high = jnp.bfloat16, jnp.float32
    window = WINDOW_TOKENS
    pairs = heads * 2 * window * TILE * 6 * factor * width
    results = pl.pallas_call(
        functools.partial(kernel, near, heads, factor),
        out_shape=[jax.ShapeDtypeStruct(x.shape, x.dtype) for x in (queries, queries, keys, values)],
        in_specs=[pl.BlockSpec(memory_space=pl.ANY)] * 4,
        out_specs=[pl.BlockSpec(memory_space=pl.ANY)] * 4,
        scratch_shapes=[
            pltpu.VMEM((heads, window, wide), low),
            pltpu.VMEM((heads, window, wide), low),
            pltpu.VMEM((heads, 2 * window, width), low),
            pltpu.VMEM((heads, 2 * window, width), low),
            pltpu.VMEM((width, 2 * window), low),
            pltpu.VMEM((width, 2 * window), low),
            pltpu.VMEM((window + TILE, factor * TILE), low),
            pltpu.VMEM((window + TILE, factor * TILE), low),
            pltpu.VMEM((heads, window, wide), low),
            pltpu.VMEM((heads, window, wide), low),
            pltpu.VMEM((heads, 2 * window, width), high),
            pltpu.VMEM((heads, 2 * window, width), high),
            *[pltpu.VMEM((heads, window, width), low)] * 6,
            pltpu.SemaphoreType.DMA((heads, members, 4)),
            pltpu.SemaphoreType.DMA((heads, members, 4)),
            *[pltpu.SemaphoreType.DMA((heads, 2))] * 2,
            *[pltpu.SemaphoreType.DMA((heads, 2, window // TILE))] * 2,
            pltpu.SemaphoreType.DMA((heads, members, 4)),
            pltpu.SemaphoreType.DMA((heads, members, 4)),
        ],
        compiler_params=pltpu.CompilerParams(
            collective_id=0, has_side_effects=True, vmem_limit_bytes=60 * 1024 * 1024
        ),
        cost_estimate=pl.CostEstimate(flops=pairs * 2, bytes_accessed=24 * queries.size, transcendentals=0),
    )(queries, keys, values, output_cotangent)
    return tuple(
        pl.pallas_call(
            hand_over,
            out_shape=[jax.ShapeDtypeStruct(x.shape, x.dtype) for x in results],
            in_specs=[pl.BlockSpec(memory_space=pl.ANY)] * 4,
            out_specs=[pl.BlockSpec(memory_space=pl.ANY)] * 4,
            scratch_shapes=[pltpu.SemaphoreType.DMA((4, 4))],
            compiler_params=pltpu.CompilerParams(vmem_limit_bytes=60 * 1024 * 1024),
        )(*results)
    )


def solution(mesh):
    spec = P(("seq", "head"), None)
    return jax.shard_map(
        body,
        mesh=mesh,
        in_specs=(spec,) * 4,
        out_specs=(spec,) * 4,
        check_vma=False,
    )
```

time: 152 us -> 336 us (2.21)
  Pallas kernels: 141 us -> 333 us
  local copies, waits for them, and re-layouts: 7.81 us -> 0 us
    pallas_call x0 -> x1, Pallas kernels: none -> 192 us  [body(): pl.pallas_call(hand_over, out_shape=[jax.ShapeDtypeStruct(x.shape, x.dtyp...]
    unnamed x10 -> x0, local copies, waits for them, and re-layouts: 7.81 us -> none
where the time goes in v2:
time: 336 us; the launch traced here: 334 us
  Pallas kernels  333 us (99%)
    pallas_call x1, Pallas kernels, body(): pl.pallas_call(hand_over, out_shape=[jax.ShapeDtypeStruct(x.shape, x.dtyp...  192 us
    pallas_call x1, Pallas kernels, body(): pl.pallas_call(functools.partial(kernel, near, heads, factor), out_shape=...  141 us

profile of v2, /device:TPU:15, one launch (start us, length us, event | category | flops | bytes accessed | tf_op | source)
XLA Modules:
  0.0 333.7 jit_solution(5490091474909484816)
XLA Ops:
  0.6 141.2 %shard_map.75 = (bf16[256,4096]{1,0:T(8,128)(2,1)}, bf16[256,4096]{1,0:T(8,128)(2,1)}, bf16[256,2048]{1,0:T(8,128)(2,1)}, bf16[256,2048]{1,0:T(8,128)(2,1)}) custom-call(bf16[256,4096]{1,0:T(8,128)(2,1)} %queries.1, bf16[256,2048]{1,0:T(8,128)(2,1)} %keys.1, bf16[256,2048]{1,0:T(8,128)(2,1)} %values.1, bf16[256,4096]{1,0:T(8,128)(2,1)} %cotangent.1), custom_call_target="tpu_custom_call" | custom-call | flops 6442450944 | bytes 25165824 | tf_op jit(solution)/shard_map/pallas_call | solution.py:351
  141.8 191.8 %shard_map.76 = (bf16[256,4096]{1,0:T(8,128)(2,1)}, bf16[256,4096]{1,0:T(8,128)(2,1)}, bf16[256,2048]{1,0:T(8,128)(2,1)}, bf16[256,2048]{1,0:T(8,128)(2,1)}) custom-call(bf16[256,4096]{1,0:T(8,128)(2,1)} %get-tuple-element.8.refs_0_, bf16[256,4096]{1,0:T(8,128)(2,1)} %get-tuple-element.9.refs_1_, bf16[256,2048]{1,0:T(8,128)(2,1)} %get-tuple-element.10.refs_2_, ...), custom_call_target="tpu_custom_call" | custom-call | tf_op jit(solution)/shard_map/pallas_call | solution.py:383

commit v3 on v2

--- a/solution.py
+++ b/solution.py
@@ -47,16 +47,18 @@
     key_at = lax.broadcasted_iota(jnp.int32, (TILE, across), 0)
     query_at = lax.broadcasted_iota(jnp.int32, (TILE, across), 1) % TILE
 
-    def block(at, _):
+    def block(at, spot):
         row = pl.multiple_of(at * TILE, TILE)
         slab = pl.ds(row, span)
         rows = [pl.ds(pl.multiple_of(row + c * TILE, TILE), TILE) for c in range(chunks + 1)]
+        here = [slice(c * TILE, (c + 1) * TILE) for c in range(chunks + 1)]
         shift = [
             jnp.where(jnp.logical_and(first, at + c < chunks), -HIDDEN, 0.0) for c in range(chunks)
         ] + [0.0]
         q = jnp.concatenate([qb[n, pl.ds(row, TILE), r * width : (r + 1) * width] for r in range(factor)], 0)
         g = jnp.concatenate([gb[n, pl.ds(row, TILE), r * width : (r + 1) * width] for r in range(factor)], 0)
         scores = []
+        top = None
         for c in range(chunks + 1):
             s = matmul_nt(kb[n, rows[c], :], q)
             if c == 0:
@@ -64,39 +66,43 @@
             if c == chunks:
                 s = jnp.where(key_at <= query_at, s, HIDDEN)
             scores.append(s)
-        top = None
-        for c in range(chunks + 1):
-            most = jnp.max(scores[c], axis=0, keepdims=True) - shift[c]
+            most = jnp.max(s, axis=0, keepdims=True) - shift[c]
             top = most if top is None else jnp.maximum(top, most)
         total = None
-        powers = []
-        for c in range(chunks + 1):
+        powers, dprobs = [], []
+        for c in range(chunks + 1):
+            dprobs.append(matmul_nt(vb[n, rows[c], :], g))
             e = jnp.exp2(scores[c] * exponent_scale - (top + shift[c]) * exponent_scale)
             part = jnp.sum(e, axis=0, keepdims=True)
             total = part if total is None else total + part
             powers.append(e)
         inverse = 1.0 / total
-        probs = [e * inverse for e in powers]
-        for c in range(chunks + 1):
-            probs_b[c * TILE : (c + 1) * TILE, :] = probs[c].astype(jnp.bfloat16)
-        out = matmul(vt[:, slab], probs_b[...])
+        probs = []
+        for c in range(chunks + 1):
+            probs.append(powers[c] * inverse)
+            probs_b[spot, here[c], :] = probs[c].astype(jnp.bfloat16)
+        out = matmul(vt[:, slab], probs_b[spot])
         out_b = out.astype(jnp.bfloat16).astype(jnp.float32)
         delta = jnp.sum(turned(g) * out_b, axis=0, keepdims=True)
         for r in range(factor):
             ob[n, pl.ds(row, TILE), r * width : (r + 1) * width] = out[:, r * TILE : (r + 1) * TILE].T.astype(jnp.bfloat16)
         for c in range(chunks + 1):
-            dprobs = matmul_nt(vb[n, rows[c], :], g)
-            dscores_b[c * TILE : (c + 1) * TILE, :] = (probs[c] * (dprobs - delta)).astype(jnp.bfloat16)
-        dq = matmul(kt[:, slab], dscores_b[...]) * query_scale
-        for c in range(chunks + 1):
-            dv[n, rows[c], :] += matmul(probs_b[c * TILE : (c + 1) * TILE, :], g)
-            dk[n, rows[c], :] += matmul(dscores_b[c * TILE : (c + 1) * TILE, :], q)
+            dscores_b[spot, here[c], :] = (probs[c] * (dprobs[c] - delta)).astype(jnp.bfloat16)
+            dv[n, rows[c], :] += matmul(probs_b[spot, here[c], :], g)
+        dq = matmul(kt[:, slab], dscores_b[spot]) * query_scale
+        for c in range(chunks + 1):
+            dk[n, rows[c], :] += matmul(dscores_b[spot, here[c], :], q)
         for r in range(factor):
             dqb[n, pl.ds(row, TILE), r * width : (r + 1) * width] = dq[:, r * TILE : (r + 1) * TILE].T.astype(jnp.bfloat16)
-        after_tile(at)
+
+    def pair(at, _):
+        block(2 * at, 0)
+        block(2 * at + 1, 1)
+        after_tile(2 * at)
+        after_tile(2 * at + 1)
         return 0
 
-    lax.fori_loop(0, (kb.shape[1] - WINDOW_TOKENS) // TILE, block, 0)
+    lax.fori_loop(0, WINDOW_TOKENS // TILE // 2, pair, 0)
 
 
 def kernel(
@@ -322,18 +328,8 @@
 
 
 def hand_over(*refs):
-    sources, targets, sems = refs[:4], refs[4:8], refs[8]
-    parts = sems.shape[1]
-    copies = []
-    for a in range(4):
-        rows = sources[a].shape[0] // parts
-        for p in range(parts):
-            piece = pl.ds(p * rows, rows)
-            copies.append(pltpu.make_async_copy(sources[a].at[piece, :], targets[a].at[piece, :], sems.at[a, p]))
-    for copy in copies:
-        copy.start()
-    for copy in copies:
-        copy.wait()
+    for source, target in zip(refs[:4], refs[4:]):
+        target[...] = source[...]
 
 
 def body(queries, keys, values, output_cotangent):
@@ -360,8 +356,8 @@
             pltpu.VMEM((heads, 2 * window, width), low),
             pltpu.VMEM((width, 2 * window), low),
             pltpu.VMEM((width, 2 * window), low),
-            pltpu.VMEM((window + TILE, factor * TILE), low),
-            pltpu.VMEM((window + TILE, factor * TILE), low),
+            pltpu.VMEM((2, window + TILE, factor * TILE), low),
+            pltpu.VMEM((2, window + TILE, factor * TILE), low),
             pltpu.VMEM((heads, window, wide), low),
             pltpu.VMEM((heads, window, wide), low),
             pltpu.VMEM((heads, 2 * window, width), high),
@@ -382,10 +378,10 @@
     return tuple(
         pl.pallas_call(
             hand_over,
+            grid=(4,),
             out_shape=[jax.ShapeDtypeStruct(x.shape, x.dtype) for x in results],
-            in_specs=[pl.BlockSpec(memory_space=pl.ANY)] * 4,
-            out_specs=[pl.BlockSpec(memory_space=pl.ANY)] * 4,
-            scratch_shapes=[pltpu.SemaphoreType.DMA((4, 4))],
+            in_specs=[pl.BlockSpec((x.shape[0] // 4, x.shape[1]), lambda i: (i, 0)) for x in results],
+            out_specs=[pl.BlockSpec((x.shape[0] // 4, x.shape[1]), lambda i: (i, 0)) for x in results],
             compiler_params=pltpu.CompilerParams(vmem_limit_bytes=60 * 1024 * 1024),
         )(*results)
     )

time: 336 us -> 150 us (0.45)
  Pallas kernels: 333 us -> 147 us
    pallas_call x1, Pallas kernels: 192 us -> 5.81 us  [body(): pl.pallas_call(hand_over, grid=(4,), out_shape=[jax.ShapeDtypeStruct(x.sh...]
where the time goes in v3:
time: 150 us; the launch traced here: 148 us
  Pallas kernels  147 us (98%)
    pallas_call x1, Pallas kernels, body(): pl.pallas_call(functools.partial(kernel, near, heads, factor), out_shape=...  141 us
    pallas_call x1, Pallas kernels, body(): pl.pallas_call(hand_over, grid=(4,), out_shape=[jax.ShapeDtypeStruct(x.sh...  5.81 us

profile of v3, /device:TPU:15, one launch (start us, length us, event | category | flops | bytes accessed | tf_op | source)
XLA Modules:
  0.0 147.6 jit_solution(10877409999722536318)
XLA Ops:
  0.6 141.2 %shard_map.75 = (bf16[256,4096]{1,0:T(8,128)(2,1)}, bf16[256,4096]{1,0:T(8,128)(2,1)}, bf16[256,2048]{1,0:T(8,128)(2,1)}, bf16[256,2048]{1,0:T(8,128)(2,1)}) custom-call(bf16[256,4096]{1,0:T(8,128)(2,1)} %queries.1, bf16[256,2048]{1,0:T(8,128)(2,1)} %keys.1, bf16[256,2048]{1,0:T(8,128)(2,1)} %values.1, bf16[256,4096]{1,0:T(8,128)(2,1)} %cotangent.1), custom_call_target="tpu_custom_call" | custom-call | flops 6442450944 | bytes 25165824 | tf_op jit(solution)/shard_map/pallas_call | solution.py:347
  141.8 5.8 %shard_map.76 = (bf16[256,4096]{1,0:T(8,128)(2,1)}, bf16[256,4096]{1,0:T(8,128)(2,1)}, bf16[256,2048]{1,0:T(8,128)(2,1)}, bf16[256,2048]{1,0:T(8,128)(2,1)}) custom-call(bf16[256,4096]{1,0:T(8,128)(2,1)} %get-tuple-element.8.refs_0_, bf16[256,4096]{1,0:T(8,128)(2,1)} %get-tuple-element.9.refs_1_, bf16[256,2048]{1,0:T(8,128)(2,1)} %get-tuple-element.10.refs_2_, ...), custom_call_target="tpu_custom_call" | custom-call | tf_op jit(solution)/shard_map/pallas_call | solution.py:379

commit v4 on v3

--- a/solution.py
+++ b/solution.py
@@ -95,14 +95,12 @@
         for r in range(factor):
             dqb[n, pl.ds(row, TILE), r * width : (r + 1) * width] = dq[:, r * TILE : (r + 1) * TILE].T.astype(jnp.bfloat16)
 
-    def pair(at, _):
-        block(2 * at, 0)
-        block(2 * at + 1, 1)
-        after_tile(2 * at)
-        after_tile(2 * at + 1)
+    def tile(at, _):
+        block(at, 0)
+        after_tile(at)
         return 0
 
-    lax.fori_loop(0, WINDOW_TOKENS // TILE // 2, pair, 0)
+    lax.fori_loop(0, WINDOW_TOKENS // TILE, tile, 0)
 
 
 def kernel(
@@ -325,11 +323,6 @@
         return 0
 
     lax.fori_loop(0, heads, drain, 0)
-
-
-def hand_over(*refs):
-    for source, target in zip(refs[:4], refs[4:]):
-        target[...] = source[...]
 
 
 def body(queries, keys, values, output_cotangent):
@@ -356,8 +349,8 @@
             pltpu.VMEM((heads, 2 * window, width), low),
             pltpu.VMEM((width, 2 * window), low),
             pltpu.VMEM((width, 2 * window), low),
-            pltpu.VMEM((2, window + TILE, factor * TILE), low),
-            pltpu.VMEM((2, window + TILE, factor * TILE), low),
+            pltpu.VMEM((1, window + TILE, factor * TILE), low),
+            pltpu.VMEM((1, window + TILE, factor * TILE), low),
             pltpu.VMEM((heads, window, wide), low),
             pltpu.VMEM((heads, window, wide), low),
             pltpu.VMEM((heads, 2 * window, width), high),
@@ -371,20 +364,11 @@
             pltpu.SemaphoreType.DMA((heads, members, 4)),
         ],
         compiler_params=pltpu.CompilerParams(
-            collective_id=0, has_side_effects=True, vmem_limit_bytes=60 * 1024 * 1024
+            collective_id=0, has_side_effects=True, vmem_limit_bytes=40 * 1024 * 1024
         ),
         cost_estimate=pl.CostEstimate(flops=pairs * 2, bytes_accessed=24 * queries.size, transcendentals=0),
     )(queries, keys, values, output_cotangent)
-    return tuple(
-        pl.pallas_call(
-            hand_over,
-            grid=(4,),
-            out_shape=[jax.ShapeDtypeStruct(x.shape, x.dtype) for x in results],
-            in_specs=[pl.BlockSpec((x.shape[0] // 4, x.shape[1]), lambda i: (i, 0)) for x in results],
-            out_specs=[pl.BlockSpec((x.shape[0] // 4, x.shape[1]), lambda i: (i, 0)) for x in results],
-            compiler_params=pltpu.CompilerParams(vmem_limit_bytes=60 * 1024 * 1024),
-        )(*results)
-    )
+    return tuple(results)
 
 
 def solution(mesh):

time: 150 us -> 154 us (1.027)
  local copies, waits for them, and re-layouts: 0 us -> 10.2 us
  Pallas kernels: 147 us -> 141 us
    unnamed x0 -> x12, local copies, waits for them, and re-layouts: none -> 10.2 us
    pallas_call x1 -> x0, Pallas kernels: 5.81 us -> none  [body(): pl.pallas_call(hand_over, grid=(4,), out_shape=[jax.ShapeDtypeStruct(x.sh...]
where the time goes in v4:
time: 154 us; the launch traced here: 152 us
  Pallas kernels  141 us (92%)
  local copies, waits for them, and re-layouts  10.2 us (7%)
    pallas_call x1, Pallas kernels, body(): pl.pallas_call(functools.partial(kernel, near, heads, factor), out_shape=...  141 us
    unnamed x12, local copies, waits for them, and re-layouts  10.2 us

profile of v4, /device:TPU:15, one launch (start us, length us, event | category | flops | bytes accessed | tf_op | source)
XLA Modules:
  0.0 151.7 jit_solution(1545440885989878223)
XLA Ops:
  0.6 0.0 copy-start
  0.6 1.6 %copy-done = bf16[256,4096]{1,0:T(8,128)(2,1)S(1)} copy-done((bf16[256,4096]{1,0:T(8,128)(2,1)S(1)}, bf16[256,4096]{1,0:T(8,128)(2,1)}, u32[]{:S(2)}) %copy-start) | copy-done | bytes 2097176
  2.2 0.0 copy-start.1
  2.2 1.6 %copy-done.1 = bf16[256,4096]{1,0:T(8,128)(2,1)S(1)} copy-done((bf16[256,4096]{1,0:T(8,128)(2,1)S(1)}, bf16[256,4096]{1,0:T(8,128)(2,1)}, u32[]{:S(2)}) %copy-start.1) | copy-done | bytes 2097176
  3.8 0.0 copy-start.2
  3.8 1.2 copy-done.2
  5.0 0.0 copy-start.3
  5.0 1.2 copy-done.3
  6.3 140.8 %shard_map.75 = (bf16[256,4096]{1,0:T(8,128)(2,1)S(1)}, bf16[256,4096]{1,0:T(8,128)(2,1)S(1)}, bf16[256,2048]{1,0:T(8,128)(2,1)S(1)}, bf16[256,2048]{1,0:T(8,128)(2,1)S(1)}) custom-call(bf16[256,4096]{1,0:T(8,128)(2,1)S(1)} %copy-done, bf16[256,2048]{1,0:T(8,128)(2,1)S(1)} %copy-done.2, bf16[256,2048]{1,0:T(8,128)(2,1)S(1)} %copy-done.3, ...), custom_call_target="tpu_custom_call" | custom-call | flops 6442450944 | bytes 25165824 | tf_op jit(solution)/shard_map/pallas_call | solution.py:340
  147.1 1.3 copy.12
  148.4 1.3 copy.13
  149.7 1.0 copy.14
  150.7 1.0 copy.15
Async XLA Ops:
  0.6 1.6 %copy-start = (bf16[256,4096]{1,0:T(8,128)(2,1)S(1)}, bf16[256,4096]{1,0:T(8,128)(2,1)}, u32[]{:S(2)}) copy-start(bf16[256,4096]{1,0:T(8,128)(2,1)} %queries.1) | copy-start | bytes 6291460
  2.2 1.6 %copy-start.1 = (bf16[256,4096]{1,0:T(8,128)(2,1)S(1)}, bf16[256,4096]{1,0:T(8,128)(2,1)}, u32[]{:S(2)}) copy-start(bf16[256,4096]{1,0:T(8,128)(2,1)} %cotangent.1) | copy-start | bytes 6291460
  3.8 1.2 copy-start.2
  5.0 1.2 copy-start.3

commit v5 on v3

--- a/solution.py
+++ b/solution.py
@@ -19,10 +19,6 @@
 
 def matmul(left, right):
     return jnp.dot(left, right, preferred_element_type=jnp.float32)
-
-
-def matmul_nt(left, right):
-    return lax.dot_general(left, right, (((1,), (1,)), ((), ())), preferred_element_type=jnp.float32)
 
 
 def turned(value):
@@ -57,10 +53,12 @@
         ] + [0.0]
         q = jnp.concatenate([qb[n, pl.ds(row, TILE), r * width : (r + 1) * width] for r in range(factor)], 0)
         g = jnp.concatenate([gb[n, pl.ds(row, TILE), r * width : (r + 1) * width] for r in range(factor)], 0)
+        g_turned = turned(g)
+        q_t, g_t = turned(q).astype(jnp.bfloat16), g_turned.astype(jnp.bfloat16)
         scores = []
         top = None
         for c in range(chunks + 1):
-            s = matmul_nt(kb[n, rows[c], :], q)
+            s = matmul(kb[n, rows[c], :], q_t)
             if c == 0:
                 s = jnp.where(key_at > query_at, s, HIDDEN)
             if c == chunks:
@@ -71,7 +69,7 @@
         total = None
         powers, dprobs = [], []
         for c in range(chunks + 1):
-            dprobs.append(matmul_nt(vb[n, rows[c], :], g))
+            dprobs.append(matmul(vb[n, rows[c], :], g_t))
             e = jnp.exp2(scores[c] * exponent_scale - (top + shift[c]) * exponent_scale)
             part = jnp.sum(e, axis=0, keepdims=True)
             total = part if total is None else total + part
@@ -83,7 +81,7 @@
             probs_b[spot, here[c], :] = probs[c].astype(jnp.bfloat16)
         out = matmul(vt[:, slab], probs_b[spot])
         out_b = out.astype(jnp.bfloat16).astype(jnp.float32)
-        delta = jnp.sum(turned(g) * out_b, axis=0, keepdims=True)
+        delta = jnp.sum(g_turned * out_b, axis=0, keepdims=True)
         for r in range(factor):
             ob[n, pl.ds(row, TILE), r * width : (r + 1) * width] = out[:, r * TILE : (r + 1) * TILE].T.astype(jnp.bfloat16)
         for c in range(chunks + 1):

time: 150 us -> 150 us (level)
  no operation moved by 1% of the time
where the time goes in v5:
time: 150 us; the launch traced here: 148 us
  Pallas kernels  147 us (98%)
    pallas_call x1, Pallas kernels, body(): pl.pallas_call(functools.partial(kernel, near, heads, factor), out_shape=...  141 us
    pallas_call x1, Pallas kernels, body(): pl.pallas_call(hand_over, grid=(4,), out_shape=[jax.ShapeDtypeStruct(x.sh...  5.81 us

profile of v5, /device:TPU:15, one launch (start us, length us, event | category | flops | bytes accessed | tf_op | source)
XLA Modules:
  0.0 147.6 jit_solution(1029284116834896280)
XLA Ops:
  0.6 141.2 %shard_map.75 = (bf16[256,4096]{1,0:T(8,128)(2,1)}, bf16[256,4096]{1,0:T(8,128)(2,1)}, bf16[256,2048]{1,0:T(8,128)(2,1)}, bf16[256,2048]{1,0:T(8,128)(2,1)}) custom-call(bf16[256,4096]{1,0:T(8,128)(2,1)} %queries.1, bf16[256,2048]{1,0:T(8,128)(2,1)} %keys.1, bf16[256,2048]{1,0:T(8,128)(2,1)} %values.1, bf16[256,4096]{1,0:T(8,128)(2,1)} %cotangent.1), custom_call_target="tpu_custom_call" | custom-call | flops 6442450944 | bytes 25165824 | tf_op jit(solution)/shard_map/pallas_call | solution.py:345
  141.8 5.8 %shard_map.76 = (bf16[256,4096]{1,0:T(8,128)(2,1)}, bf16[256,4096]{1,0:T(8,128)(2,1)}, bf16[256,2048]{1,0:T(8,128)(2,1)}, bf16[256,2048]{1,0:T(8,128)(2,1)}) custom-call(bf16[256,4096]{1,0:T(8,128)(2,1)} %get-tuple-element.8.refs_0_, bf16[256,4096]{1,0:T(8,128)(2,1)} %get-tuple-element.9.refs_1_, bf16[256,2048]{1,0:T(8,128)(2,1)} %get-tuple-element.10.refs_2_, ...), custom_call_target="tpu_custom_call" | custom-call | tf_op jit(solution)/shard_map/pallas_call | solution.py:377
